TPU v7x, 512 devices: a whole 4x4x16 slice. The times are simulated.
512 devices in a mesh: dp: 8 (over y, core), space: 64 (over x, z).
Axes of the slice: x: 4, y: 4, z: 16, core: 2. Of those that a mesh axis runs over, the one named last changes fastest.
Arguments:
- fine_features: bfloat16 [8, 1536, 4, 4, 256], P('dp', 'space'), may hold values from -6 to 6
- cotangent: bfloat16 [8, 1536, 4, 4, 256], P('dp', 'space'), may hold values from -0.01953125 to 0.01953125
- down_weight: bfloat16 [1728, 128], replicated, may hold values from -0.15625 to 0.15625
- coarse_weight: bfloat16 [3456, 128], replicated, may hold values from -0.109375 to 0.109375
- up_weight: bfloat16 [128, 512], replicated, may hold values from -0.5 to 0.5
- fine_neighbours: int32 [8, 1536, 7], P('dp', 'space'), may hold values from -1 to 1535, as said below
- children: int32 [8, 384, 8], P('dp', 'space'), may hold values from -1 to 1535, as said below
- parent_slots: int32 [8, 1536], P('dp', 'space'), may hold values from 0 to 3071, as said below
- coarse_neighbours: int32 [8, 384, 26], P('dp', 'space'), may hold values from -1 to 383, as said below
Outputs:
- decoded: bfloat16 [8, 1536, 4, 4, 256], P('dp', 'space')
- grad_down: float32 [221184], P('space')
- grad_coarse: float32 [442368], P('space')
- grad_up: float32 [65536], P('space')
Inputs may be any that keep to these rules, and one draw needn't show every extreme that they name: Bricks sit in a strip of the map with coordinates; fine_neighbours lists the occupied brick at the named lower offset. Every listed neighbour of fine brick f is lower than f and at least 24 * (f // 24 - 1). Each coarse brick has 3 to 5 children; children[t, c, o] = f exactly when parent_slots[t, f] = 8 c + o, and every fine brick is the child of one coarse brick. The children of coarse brick c lie from 24 * (c // 6) to 24 * (c // 6 + 1), both included. `parent_slots`: the parent of fine brick f is a coarse brick from 6 * (f // 24) to 6 * (f // 24 + 1) - 1, or the coarse brick 6 * (f // 24) - 1. `coarse_neighbours`: Symmetric: if the entry of c for offset (sx, sy, sz) is d, the entry of d for the opposite offset is c. Coarse brick c lies in cross-section c // 2 of the strip, and a listed neighbour of c for offset (sx, sy, sz) lies in cross-section c // 2 + sx.
All inputs are finite; a program needn't handle non-finite values.
Results may differ from a plain program's by a relative error of at most 0.0065.
The roundings to bfloat16 on the way count: a program that leaves them out, or rounds other values in their place, can miss the bound.
Values may be sent and summed in bfloat16 or wider, within the bound.
No kernel may reach another device: no remote copies, remote signals or barrier semaphores. Data moves between devices by JAX's collectives and lax.ppermute only.
A program may use at most 64 MiB of HBM per device.

v0:
```python
import jax
import jax.numpy as jnp
from jax import lax
from jax.sharding import PartitionSpec as P


def padded_2(x, sides, width):
    for axis, dim in sides:
        size, length = (lax.axis_size(axis), x.shape[dim])
        up = [(i, (i + 1) % size) for i in range(size - 1)]
        down = [(j, i) for i, j in up]
        last = lax.slice_in_dim(x, length - width, length, axis=dim)
        leading = lax.slice_in_dim(x, 0, width, axis=dim)
        before = lax.ppermute(last, axis, up)
        after = lax.ppermute(leading, axis, down)
        x = jnp.concatenate([before, x, after], axis=dim)
    return x


def from_behind(block, axis, distance):
    devices = range(lax.axis_size(axis))
    route = [(i - distance, i) for i in devices if i - distance in devices]
    return lax.ppermute(block, axis, route)


def silu_slope(inputs):
    squash = jax.nn.sigmoid(inputs)
    return squash * (1.0 + inputs * (1.0 - squash))


def edge_pick(offset_value, brick_edge):
    if offset_value < 0:
        return slice(brick_edge - 1, brick_edge)
    if offset_value > 0:
        return slice(0, 1)
    return slice(0, brick_edge)


def edge_place(offset_value, brick_edge):
    if offset_value < 0:
        return slice(0, 1)
    if offset_value > 0:
        return slice(brick_edge + 1, brick_edge + 2)
    return slice(1, brick_edge + 1)


def fine_planes(bricks):
    return jnp.stack([bricks[:, -1], bricks[:, :, -1], bricks[:, :, :, -1]], axis=1)


def fine_padded(bricks, planes_all, neighbours):
    brick_edge = bricks.shape[1]
    padded = jnp.pad(bricks, ((0, 0), (1, 0), (1, 0), (1, 0), (0, 0)))
    for bit_code in range(1, 8):
        shift_x = bit_code // 4
        shift_y = bit_code // 2 % 2
        shift_z = bit_code % 2
        picked = planes_all[neighbours[:, bit_code - 1]]
        if shift_x:
            values = picked[:, 0][
                :, edge_pick(-shift_y, brick_edge), edge_pick(-shift_z, brick_edge)
            ][:, None]
        elif shift_y:
            values = picked[:, 1][:, :, edge_pick(-shift_z, brick_edge)][:, :, None]
        else:
            values = picked[:, 2][:, :, :, None]
        place_x = slice(0, 1) if shift_x else slice(1, brick_edge + 1)
        place_y = slice(0, 1) if shift_y else slice(1, brick_edge + 1)
        place_z = slice(0, 1) if shift_z else slice(1, brick_edge + 1)
        padded = padded.at[:, place_x, place_y, place_z].set(values)
    return padded


def fine_columns(padded, half_edge):
    tap_list = []
    for tap_code in range(27):
        along_x = tap_code // 9
        along_y = tap_code // 3 % 3
        along_z = tap_code % 3
        tap_list.append(
            padded[
                :,
                along_x : along_x + 2 * half_edge - 1 : 2,
                along_y : along_y + 2 * half_edge - 1 : 2,
                along_z : along_z + 2 * half_edge - 1 : 2,
            ]
        )
    stacked = jnp.stack(tap_list, axis=4)
    return stacked.reshape(-1, 27 * stacked.shape[-1])


def octants_to_bricks(patches):
    brick_count = patches.shape[0]
    half_edge = patches.shape[2]
    channels = patches.shape[-1]
    arranged = patches.reshape(brick_count, 2, 2, 2, half_edge, half_edge, half_edge, channels)
    arranged = arranged.transpose(0, 1, 4, 2, 5, 3, 6, 7)
    return arranged.reshape(brick_count, 2 * half_edge, 2 * half_edge, 2 * half_edge, channels)


def bricks_to_octants(bricks):
    brick_count = bricks.shape[0]
    half_edge = bricks.shape[1] // 2
    channels = bricks.shape[-1]
    arranged = bricks.reshape(brick_count, 2, half_edge, 2, half_edge, 2, half_edge, channels)
    arranged = arranged.transpose(0, 1, 3, 5, 2, 4, 6, 7)
    return arranged.reshape(brick_count * 8, half_edge, half_edge, half_edge, channels)


def coarse_faces(bricks):
    return jnp.stack(
        [
            bricks[:, 0],
            bricks[:, -1],
            bricks[:, :, 0],
            bricks[:, :, -1],
            bricks[:, :, :, 0],
            bricks[:, :, :, -1],
        ],
        axis=1,
    )


def coarse_padded(bricks, faces_all, neighbours):
    brick_edge = bricks.shape[1]
    padded = jnp.pad(bricks, ((0, 0), (1, 1), (1, 1), (1, 1), (0, 0)))
    offset_codes = [offset_code for offset_code in range(27) if offset_code != 13]
    for column_index, offset_code in enumerate(offset_codes):
        off_x = offset_code // 9 - 1
        off_y = offset_code // 3 % 3 - 1
        off_z = offset_code % 3 - 1
        picked = faces_all[neighbours[:, column_index]]
        if off_x != 0:
            values = picked[:, 1 if off_x < 0 else 0][
                :, edge_pick(off_y, brick_edge), edge_pick(off_z, brick_edge)
            ][:, None]
        elif off_y != 0:
            values = picked[:, 3 if off_y < 0 else 2][:, :, edge_pick(off_z, brick_edge)][
                :, :, None
            ]
        else:
            values = picked[:, 5 if off_z < 0 else 4][:, :, :, None]
        padded = padded.at[
            :,
            edge_place(off_x, brick_edge),
            edge_place(off_y, brick_edge),
            edge_place(off_z, brick_edge),
        ].set(values)
    return padded


def pair_taps(padded, along_x, along_y, reverse):
    brick_edge = padded.shape[1] - 2
    pieces = []
    for along_z in range(3):
        if reverse:
            lows = (2 - along_x, 2 - along_y, 2 - along_z)
        else:
            lows = (along_x, along_y, along_z)
        pieces.append(
            padded[
                :,
                lows[0] : lows[0] + brick_edge,
                lows[1] : lows[1] + brick_edge,
                lows[2] : lows[2] + brick_edge,
            ]
        )
    gathered_taps = jnp.concatenate(pieces, axis=-1)
    return gathered_taps.reshape(-1, gathered_taps.shape[-1])


def coarse_forward(padded, weight):
    channels = weight.shape[0] // 27
    summed = None
    for pair_code in range(9):
        gathered_taps = pair_taps(padded, pair_code // 3, pair_code % 3, False)
        weight_rows = weight[pair_code * 3 * channels : (pair_code + 1) * 3 * channels]
        partial_value = jnp.dot(gathered_taps, weight_rows, preferred_element_type=jnp.float32)
        summed = partial_value if summed is None else summed + partial_value
    return summed


def coarse_weight_grad(padded, slope_rows):
    blocks = []
    for pair_code in range(9):
        gathered_taps = pair_taps(padded, pair_code // 3, pair_code % 3, False)
        blocks.append(
            lax.dot_general(
                gathered_taps,
                slope_rows,
                (((0,), (0,)), ((), ())),
                preferred_element_type=jnp.float32,
            )
        )
    return jnp.concatenate(blocks, axis=0)


def coarse_transpose(padded, weight):
    channels_in = weight.shape[0] // 27
    channels_out = weight.shape[1]
    summed = None
    for pair_code in range(9):
        gathered_taps = pair_taps(padded, pair_code // 3, pair_code % 3, True)
        weight_block = weight[pair_code * 3 * channels_in : (pair_code + 1) * 3 * channels_in]
        weight_block = (
            weight_block.reshape(3, channels_in, channels_out)
            .transpose(0, 2, 1)
            .reshape(3 * channels_out, channels_in)
        )
        partial_value = jnp.dot(gathered_taps, weight_block, preferred_element_type=jnp.float32)
        summed = partial_value if summed is None else summed + partial_value
    return summed


def wide_faces(faces_own, forward):
    count = faces_own.shape[0]
    if forward:
        return padded_2(faces_own, (("space", 0),), count)
    return padded_2(faces_own, (("space", 0),), count)


def parent_patches(octants, parent_list, place_index, forward):
    patch_count = octants.shape[0]
    half_edge = octants.shape[1]
    channels = octants.shape[-1]
    tail_octants = octants[patch_count - 8 :].reshape(8, half_edge, half_edge, half_edge * channels)
    if forward:
        arrived = from_behind(tail_octants, "space", 1)
    else:
        arrived = from_behind(tail_octants, "space", 1)
    patch_pool = jnp.concatenate(
        [arrived.reshape(8, half_edge, half_edge, half_edge, channels), octants], axis=0
    )
    offset_slot = (patch_count // 8 * place_index - 1) * 8
    return patch_pool[parent_list - offset_slot]


def body(
    fine_features,
    cotangent,
    down_weight,
    coarse_weight,
    up_weight,
    fine_neighbours,
    children,
    parent_slots,
    coarse_neighbours,
):
    place_index = lax.axis_index("space")
    brick_edge = fine_features.shape[2]
    half_edge = brick_edge // 2
    fine_width = down_weight.shape[0] // 27
    coarse_width = down_weight.shape[1]
    fine_count = fine_features.shape[1]
    coarse_count = children.shape[1]
    bricks = fine_features.reshape(fine_count, brick_edge, brick_edge, brick_edge, fine_width)
    own_planes = fine_planes(bricks).reshape(fine_count, 3, brick_edge, brick_edge * fine_width)
    prev_planes = from_behind(own_planes, "space", 1)
    zero_planes = jnp.zeros((1, 3, brick_edge, brick_edge * fine_width), jnp.bfloat16)
    planes_all = jnp.concatenate([prev_planes, own_planes, zero_planes], axis=0)
    planes_all = planes_all.reshape(2 * fine_count + 1, 3, brick_edge, brick_edge, fine_width)
    fine_nbr = fine_neighbours[0]
    local_fine = jnp.where(fine_nbr < 0, 2 * fine_count, fine_nbr - fine_count * (place_index - 1))
    padded_fine = fine_padded(bricks, planes_all, local_fine)
    columns = fine_columns(padded_fine, half_edge)
    pre_down = jnp.dot(columns, down_weight, preferred_element_type=jnp.float32)
    hidden = jax.nn.silu(pre_down).astype(jnp.bfloat16)
    patches = hidden.reshape(fine_count, half_edge, half_edge, half_edge * coarse_width)
    next_first = from_behind(patches[0:1], "space", -1)
    zero_patch = jnp.zeros((1, half_edge, half_edge, half_edge * coarse_width), jnp.bfloat16)
    patch_pool = jnp.concatenate([patches, next_first, zero_patch], axis=0)
    patch_pool = patch_pool.reshape(fine_count + 2, half_edge, half_edge, half_edge, coarse_width)
    child_list = children[0]
    child_local = jnp.where(child_list < 0, fine_count + 1, child_list - fine_count * place_index)
    coarse_in = octants_to_bricks(patch_pool[child_local])
    coarse_nbr = coarse_neighbours[0]
    local_coarse = jnp.where(
        coarse_nbr < 0, 3 * coarse_count, coarse_nbr - coarse_count * (place_index - 1)
    )
    zero_faces = jnp.zeros((1, 6, brick_edge, brick_edge * coarse_width), jnp.bfloat16)
    faces_own = coarse_faces(coarse_in).reshape(
        coarse_count, 6, brick_edge, brick_edge * coarse_width
    )
    faces_wide = wide_faces(faces_own, True)
    faces_all = jnp.concatenate([faces_wide, zero_faces], axis=0)
    faces_all = faces_all.reshape(3 * coarse_count + 1, 6, brick_edge, brick_edge, coarse_width)
    padded_in = coarse_padded(coarse_in, faces_all, local_coarse)
    pre_coarse = coarse_forward(padded_in, coarse_weight)
    coarse_out = jax.nn.silu(pre_coarse).astype(jnp.bfloat16)
    coarse_out = coarse_out.reshape(coarse_count, brick_edge, brick_edge, brick_edge, coarse_width)
    parent_list = parent_slots[0]
    up_input = parent_patches(bricks_to_octants(coarse_out), parent_list, place_index, True)
    up_rows = up_input.reshape(-1, coarse_width)
    up_out = jnp.dot(up_rows, up_weight, preferred_element_type=jnp.float32)
    up_grid = up_out.reshape(
        fine_count, half_edge, half_edge, half_edge, 2, 2, 2, fine_width
    ).transpose(0, 1, 4, 2, 5, 3, 6, 7)
    up_grid = up_grid.reshape(fine_count, brick_edge, brick_edge, brick_edge, fine_width)
    joined = up_grid + bricks.astype(jnp.float32)
    decoded = jax.nn.silu(joined).astype(jnp.bfloat16).reshape(fine_features.shape)
    cot_grid = cotangent.reshape(fine_count, brick_edge, brick_edge, brick_edge, fine_width).astype(
        jnp.float32
    )
    out_grad = (cot_grid * silu_slope(joined)).astype(jnp.bfloat16)
    out_rows = out_grad.reshape(
        fine_count, half_edge, 2, half_edge, 2, half_edge, 2, fine_width
    ).transpose(0, 1, 3, 5, 2, 4, 6, 7)
    out_rows = out_rows.reshape(-1, 8 * fine_width)
    grad_up = lax.dot_general(
        up_rows, out_rows, (((0,), (0,)), ((), ())), preferred_element_type=jnp.float32
    )
    patch_grad = lax.dot_general(
        out_rows, up_weight, (((1,), (1,)), ((), ())), preferred_element_type=jnp.float32
    ).astype(jnp.bfloat16)
    grad_patches = patch_grad.reshape(fine_count, half_edge, half_edge, half_edge * coarse_width)
    next_grad = from_behind(grad_patches[0:1], "space", -1)
    grad_pool = jnp.concatenate([grad_patches, next_grad, zero_patch], axis=0)
    grad_pool = grad_pool.reshape(fine_count + 2, half_edge, half_edge, half_edge, coarse_width)
    coarse_grad_out = octants_to_bricks(grad_pool[child_local])
    coarse_slope = (
        coarse_grad_out.reshape(-1, coarse_width).astype(jnp.float32) * silu_slope(pre_coarse)
    ).astype(jnp.bfloat16)
    grad_coarse = coarse_weight_grad(padded_in, coarse_slope)
    slope_bricks = coarse_slope.reshape(
        coarse_count, brick_edge, brick_edge, brick_edge, coarse_width
    )
    slope_faces = coarse_faces(slope_bricks).reshape(
        coarse_count, 6, brick_edge, brick_edge * coarse_width
    )
    slope_wide = wide_faces(slope_faces, False)
    slope_all = jnp.concatenate([slope_wide, zero_faces], axis=0)
    slope_all = slope_all.reshape(3 * coarse_count + 1, 6, brick_edge, brick_edge, coarse_width)
    padded_slope = coarse_padded(slope_bricks, slope_all, local_coarse)
    input_grad = coarse_transpose(padded_slope, coarse_weight).astype(jnp.bfloat16)
    input_bricks = input_grad.reshape(
        coarse_count, brick_edge, brick_edge, brick_edge, coarse_width
    )
    hidden_grad = parent_patches(bricks_to_octants(input_bricks), parent_list, place_index, False)
    down_slope = (
        hidden_grad.reshape(-1, coarse_width).astype(jnp.float32) * silu_slope(pre_down)
    ).astype(jnp.bfloat16)
    grad_down = lax.dot_general(
        columns, down_slope, (((0,), (0,)), ((), ())), preferred_element_type=jnp.float32
    )
    flat_down = grad_down.reshape(-1)
    flat_coarse = grad_coarse.reshape(-1)
    flat_up = grad_up.reshape(-1)
    whole_down, whole_coarse, whole_up = lax.psum(
        (flat_down, flat_coarse, flat_up), ("dp", "space")
    )
    space_count = lax.axis_size("space")
    share_down = lax.dynamic_slice_in_dim(
        whole_down,
        place_index * (flat_down.shape[0] // space_count),
        flat_down.shape[0] // space_count,
    )
    share_coarse = lax.dynamic_slice_in_dim(
        whole_coarse,
        place_index * (flat_coarse.shape[0] // space_count),
        flat_coarse.shape[0] // space_count,
    )
    share_up = lax.dynamic_slice_in_dim(
        whole_up, place_index * (flat_up.shape[0] // space_count), flat_up.shape[0] // space_count
    )
    return (decoded, share_down, share_coarse, share_up)


def solution(mesh):
    in_specs = (
        P("dp", "space", None, None, None),
        P("dp", "space", None, None, None),
        P(),
        P(),
        P(),
        P("dp", "space", None),
        P("dp", "space", None),
        P("dp", "space"),
        P("dp", "space", None),
    )
    out_specs = (P("dp", "space", None, None, None), P("space"), P("space"), P("space"))
    return jax.shard_map(body, mesh=mesh, in_specs=in_specs, out_specs=out_specs, check_vma=False)
```

profile of v0, /device:TPU:2, one launch (start us, length us, event | category | flops | bytes accessed | tf_op | source)
XLA Modules:
  0.0 735.8 jit_solution(11911529440482196568)
XLA Ops:
  7.2 1.8 copy_convert_fusion
  10.0 3.8 collective-permute-start
  15.8 9.5 %collective-permute-done = bf16[24,3,4,256]{3,0,2,1:T(8,128)(2,1)S(1)} collective-permute-done((bf16[24,3,4,256]{3,0,2,1:T(8,128)(2,1)S(1)}, bf16[24,3,4,256]{3,0,2,1:T(8,128)(2,1)S(1)}, u32[]{:S(2)}, u32[]{:S(2)}) %collective-permute-start) | collective-permute-done | bytes 147488 | tf_op jit(solution)/shard_map/ppermute | solution.py:23
  32.3 7.6 %scatter.196 = bf16[24,5,5,5,64]{4,3,0,2,1:T(8,128)(2,1)S(1)} dynamic-update-slice(bf16[24,5,5,5,64]{4,3,0,2,1:T(8,128)(2,1)S(1)} %pad.247, bf16[24,4,4,1,64]{4,3,0,2,1:T(2,128)(2,1)S(1)} %copy.350, s32[]{:T(128)} %constant.1608.clone.1, s32[]{:T(128)} %constant.1614.clone.1, s32[]{:T(128)} %constant.1614.clone.1, s32[]{:T(128)} %constant.1608.clone.1, s32[]{:T(128)} %constant.1608.clone.1) | dynamic-update-slice | bytes 98308 | tf_op jit(solution)/shard_map/scatter | solution.py:70
  39.9 3.1 scatter.199
  44.7 3.4 scatter.201
  48.2 1.9 scatter.204
  62.0 3.6 collective-permute-start.1
  69.1 5.8 collective-permute-start.3
  74.8 1.9 collective-permute-start.2
  77.5 6.5 collective-permute-done.2
  113.0 2.0 pad_maximum_fusion.7
  116.7 1.8 pad_maximum_fusion.8
  123.6 2.1 collective-permute-start.4
  142.5 6.4 collective-permute-start.5
  151.9 6.3 collective-permute-start.7
  158.2 1.9 collective-permute-start.6
  163.7 3.7 collective-permute-done.6
  226.8 1.9 pad_maximum_fusion.16
  229.7 1.8 pad_maximum_fusion.17
  231.5 1.8 reshape.3031
  237.8 1.9 collective-permute-start.8
  240.8 4.8 collective-permute-done.8
  249.8 474.9 %all-reduce.6.cloned.1.call-done = (f32[221184]{0:T(1024)}, f32[442368]{0:T(1024)}, f32[65536]{0:T(1024)}) async-done(((f32[221184]{0:T(1024)}, f32[442368]{0:T(1024)}, f32[65536]{0:T(1024)}), (f32[221184]{0:T(1024)}, f32[442368]{0:T(1024)}, f32[65536]{0:T(1024)})) %all-reduce.6.cloned.1.call-update) | async-done | bytes 2916368 | tf_op jit(solution)/shard_map/psum | solution.py:348
  (635 shorter events, 157.7 us)
Async XLA Ops:
  7.2 717.5 %all-reduce.6.cloned.1.call-start = ((), (), s32[]{:S(2)}) async-start(), calls=%async_computation | async-start | bytes 5832704 | tf_op jit(solution)/shard_map/psum | solution.py:348
  10.0 15.2 %collective-permute-start = (bf16[24,3,4,256]{3,0,2,1:T(8,128)(2,1)S(1)}, bf16[24,3,4,256]{3,0,2,1:T(8,128)(2,1)S(1)}, u32[]{:S(2)}, u32[]{:S(2)}) collective-permute-start(bf16[24,3,4,256]{3,0,2,1:T(8,128)(2,1)S(1)} %constant_dynamic-update-slice_fusion), channel_id=1, source_target_pairs={{0,1},{1,2},{2,3},{3,4},{4,5},{5,6},{6,7},{7,8},{8,9},{9,10},{10,1... | collective-permute-start | bytes 442376 | tf_op jit(solution)/shard_map/ppermute | solution.py:23
  15.0 76.2 %copy-start.46 = (s32[1024]{0:T(1024)}, s32[1024]{0:T(1024)S(1)}, u32[]{:S(2)}) copy-start(s32[1024]{0:T(1024)S(1)} %get-tuple-element.872) | copy-start | bytes 12292
  15.0 76.9 %copy-start.45 = (s32[1024]{0:T(1024)}, s32[1024]{0:T(1024)S(1)}, u32[]{:S(2)}) copy-start(s32[1024]{0:T(1024)S(1)} %get-tuple-element.871) | copy-start | bytes 12292
  15.0 77.6 %copy-start.48 = (s32[1024]{0:T(1024)}, s32[1024]{0:T(1024)S(1)}, u32[]{:S(2)}) copy-start(s32[1024]{0:T(1024)S(1)} %get-tuple-element.870) | copy-start | bytes 12292
  15.0 78.3 %copy-start.47 = (s32[1024]{0:T(1024)}, s32[1024]{0:T(1024)S(1)}, u32[]{:S(2)}) copy-start(s32[1024]{0:T(1024)S(1)} %get-tuple-element.869) | copy-start | bytes 12292
  15.1 79.1 %copy-start.50 = (s32[1024]{0:T(1024)}, s32[1024]{0:T(1024)S(1)}, u32[]{:S(2)}) copy-start(s32[1024]{0:T(1024)S(1)} %get-tuple-element.868) | copy-start | bytes 12292
  15.1 79.8 %copy-start.49 = (s32[1024]{0:T(1024)}, s32[1024]{0:T(1024)S(1)}, u32[]{:S(2)}) copy-start(s32[1024]{0:T(1024)S(1)} %get-tuple-element.867) | copy-start | bytes 12292
  15.1 80.5 %copy-start.52 = (s32[1024]{0:T(1024)}, s32[1024]{0:T(1024)S(1)}, u32[]{:S(2)}) copy-start(s32[1024]{0:T(1024)S(1)} %get-tuple-element.866) | copy-start | bytes 12292
  15.1 81.2 %copy-start.51 = (s32[1024]{0:T(1024)}, s32[1024]{0:T(1024)S(1)}, u32[]{:S(2)}) copy-start(s32[1024]{0:T(1024)S(1)} %get-tuple-element.865) | copy-start | bytes 12292
  15.1 82.0 %copy-start.54 = (s32[1024]{0:T(1024)}, s32[1024]{0:T(1024)S(1)}, u32[]{:S(2)}) copy-start(s32[1024]{0:T(1024)S(1)} %get-tuple-element.864) | copy-start | bytes 12292
  15.1 82.7 %copy-start.53 = (s32[1024]{0:T(1024)}, s32[1024]{0:T(1024)S(1)}, u32[]{:S(2)}) copy-start(s32[1024]{0:T(1024)S(1)} %get-tuple-element.863) | copy-start | bytes 12292
  15.2 83.4 %copy-start.56 = (s32[1024]{0:T(1024)}, s32[1024]{0:T(1024)S(1)}, u32[]{:S(2)}) copy-start(s32[1024]{0:T(1024)S(1)} %get-tuple-element.862) | copy-start | bytes 12292
  15.2 84.1 %copy-start.55 = (s32[1024]{0:T(1024)}, s32[1024]{0:T(1024)S(1)}, u32[]{:S(2)}) copy-start(s32[1024]{0:T(1024)S(1)} %get-tuple-element.861) | copy-start | bytes 12292
  15.7 84.3 %copy-start.58 = (s32[1024]{0:T(1024)}, s32[1024]{0:T(1024)S(1)}, u32[]{:S(2)}) copy-start(s32[1024]{0:T(1024)S(1)} %get-tuple-element.860) | copy-start | bytes 12292
  15.8 85.0 %copy-start.57 = (s32[1024]{0:T(1024)}, s32[1024]{0:T(1024)S(1)}, u32[]{:S(2)}) copy-start(s32[1024]{0:T(1024)S(1)} %get-tuple-element.859) | copy-start | bytes 12292
  62.0 5.5 collective-permute-start.1
  69.1 8.4 %collective-permute-start.3 = (bf16[6,6,4,512]{3,2,0,1:T(4,128)(2,1)S(1)}, bf16[6,6,4,512]{3,2,0,1:T(4,128)(2,1)S(1)}, u32[]{:S(2)}, u32[]{:S(2)}) collective-permute-start(bf16[6,6,4,512]{3,2,0,1:T(4,128)(2,1)S(1)} %constant_dynamic-update-slice_fusion.30), channel_id=1, source_target_pairs={{1,0},{2,1},{3,2},{4,3},{5,4},{6,5},{7,6},{8,7},{9,8},{10,9},{11,1... | collective-permute-start | bytes 442376 | tf_op jit(solution)/shard_map/ppermute | solution.py:15
  74.8 9.1 %collective-permute-start.2 = (bf16[6,6,4,512]{3,2,0,1:T(4,128)(2,1)S(1)}, bf16[6,6,4,512]{3,2,0,1:T(4,128)(2,1)S(1)}, u32[]{:S(2)}, u32[]{:S(2)}) collective-permute-start(bf16[6,6,4,512]{3,2,0,1:T(4,128)(2,1)S(1)} %constant_dynamic-update-slice_fusion.30), channel_id=1, source_target_pairs={{0,1},{1,2},{2,3},{3,4},{4,5},{5,6},{6,7},{7,8},{8,9},{9,10},{10,1... | collective-permute-start | bytes 442376 | tf_op jit(solution)/shard_map/ppermute | solution.py:14
  123.6 15.2 %collective-permute-start.4 = (bf16[8,2,2,256]{3,0,2,1:T(8,128)(2,1)S(1)}, bf16[8,2,2,256]{3,0,2,1:T(8,128)(2,1)S(1)}, u32[]{:S(2)}, u32[]{:S(2)}) collective-permute-start(bf16[8,2,2,256]{3,0,2,1:T(8,128)(2,1)S(1)} %bitcast.517), channel_id=1, source_target_pairs={{0,1},{1,2},{2,3},{3,4},{4,5},{5,6},{6,7},{7,8},{8,9},{9,10},{10,1... | collective-permute-start | bytes 49160 | tf_op jit(solution)/shard_map/ppermute | solution.py:23
  142.5 7.4 %collective-permute-start.5 = (bf16[1,2,2,256]{3,2,1,0:T(2,128)(2,1)S(1)}, bf16[1,2,2,256]{3,2,1,0:T(2,128)(2,1)S(1)}, u32[]{:S(2)}, u32[]{:S(2)}) collective-permute-start(bf16[1,2,2,256]{3,2,1,0:T(2,128)(2,1)S(1)} %slice.3357), channel_id=1, source_target_pairs={{1,0},{2,1},{3,2},{4,3},{5,4},{6,5},{7,6},{8,7},{9,8},{10,9},{11,1... | collective-permute-start | bytes 6152 | tf_op jit(solution)/shard_map/ppermute | solution.py:23
  151.9 11.8 %collective-permute-start.7 = (bf16[6,6,4,512]{3,2,0,1:T(4,128)(2,1)S(1)}, bf16[6,6,4,512]{3,2,0,1:T(4,128)(2,1)S(1)}, u32[]{:S(2)}, u32[]{:S(2)}) collective-permute-start(bf16[6,6,4,512]{3,2,0,1:T(4,128)(2,1)S(1)} %constant_dynamic-update-slice_fusion.36), channel_id=1, source_target_pairs={{1,0},{2,1},{3,2},{4,3},{5,4},{6,5},{7,6},{8,7},{9,8},{10,9},{11,1... | collective-permute-start | bytes 442376 | tf_op jit(solution)/shard_map/ppermute | solution.py:15
  158.2 9.1 %collective-permute-start.6 = (bf16[6,6,4,512]{3,2,0,1:T(4,128)(2,1)S(1)}, bf16[6,6,4,512]{3,2,0,1:T(4,128)(2,1)S(1)}, u32[]{:S(2)}, u32[]{:S(2)}) collective-permute-start(bf16[6,6,4,512]{3,2,0,1:T(4,128)(2,1)S(1)} %constant_dynamic-update-slice_fusion.36), channel_id=1, source_target_pairs={{0,1},{1,2},{2,3},{3,4},{4,5},{5,6},{6,7},{7,8},{8,9},{9,10},{10,1... | collective-permute-start | bytes 442376 | tf_op jit(solution)/shard_map/ppermute | solution.py:14
  237.8 7.7 %collective-permute-start.8 = (bf16[8,2,2,256]{3,0,2,1:T(8,128)(2,1)S(1)}, bf16[8,2,2,256]{3,0,2,1:T(8,128)(2,1)S(1)}, u32[]{:S(2)}, u32[]{:S(2)}) collective-permute-start(bf16[8,2,2,256]{3,0,2,1:T(8,128)(2,1)S(1)} %bitcast.518), channel_id=1, source_target_pairs={{0,1},{1,2},{2,3},{3,4},{4,5},{5,6},{6,7},{7,8},{8,9},{9,10},{10,1... | collective-permute-start | bytes 49160 | tf_op jit(solution)/shard_map/ppermute | solution.py:23
  (58 other events, 844.1 us)
Sparse Core Ops, SparseCore 0:
  248.0 476.6 all-reduce.5
where the time goes:
time: 745 us; the launch traced here: 736 us
  waiting for transfers between devices  502 us (67%)
  local copies, waits for them, and re-layouts  151 us (20%)
  starting transfers between devices  33.8 us (5%)
  between operations  18 us (2%)
  other arithmetic  17.7 us (2%)
  matrix products  14 us (2%)
    psum x1, waiting for transfers between devices, body(): lax.psum((flat_down, flat_coarse, flat_up), ('dp', 'space'))  475 us
    gather x52, local copies, waits for them, and re-layouts, coarse_padded(): picked = faces_all[neighbours[:, column_index]]  50 us
    scatter x7, local copies, waits for them, and re-layouts, fine_padded(): padded = padded.at[:, place_x, place_y, place_z].set(values)  18.1 us
    ppermute x5, starting transfers between devices, from_behind(): return lax.ppermute(block, axis, route)  17.9 us
    ppermute x5, waiting for transfers between devices, from_behind(): return lax.ppermute(block, axis, route)  16 us
  transfers between devices with their start and end apart: 10, of which 7 were waited for; matrix products, arithmetic and copies ran while one was open for 3% of the time, Pallas kernels for 0%

commit v1 on v0

--- a/solution.py
+++ b/solution.py
@@ -346,7 +346,7 @@
     flat_coarse = grad_coarse.reshape(-1)
     flat_up = grad_up.reshape(-1)
     whole_down, whole_coarse, whole_up = lax.psum(
-        (flat_down, flat_coarse, flat_up), ("dp", "space")
+        lax.psum((flat_down, flat_coarse, flat_up), "space"), "dp"
     )
     space_count = lax.axis_size("space")
     share_down = lax.dynamic_slice_in_dim(

time: 745 us -> 625 us (0.84)
  waiting for transfers between devices: 502 us -> 382 us
    psum x1 -> x2, waiting for transfers between devices: 475 us -> 355 us  [the longest x1 274 us: body(): lax.psum((flat_down, flat_coarse, flat_up), 'space')]
  transfers between devices with their start and end apart: 10 -> 11, of which waited for: 7 -> 8; matrix products, arithmetic and copies ran while one was open for 3% -> 3% of each run, Pallas kernels for 0% -> 0%
where the time goes in v1:
time: 625 us; the launch traced here: 616 us
  waiting for transfers between devices  382 us (61%)
  local copies, waits for them, and re-layouts  151 us (24%)
  starting transfers between devices  33.8 us (5%)
  between operations  18 us (3%)
  other arithmetic  17.8 us (3%)
  matrix products  14.1 us (2%)
    psum x1, waiting for transfers between devices, body(): lax.psum((flat_down, flat_coarse, flat_up), 'space')  274 us
    psum x1, waiting for transfers between devices, body(): lax.psum(lax.psum((flat_down, flat_coarse, flat_up), 'space'), 'dp')  81 us
    gather x52, local copies, waits for them, and re-layouts, coarse_padded(): picked = faces_all[neighbours[:, column_index]]  50 us
    scatter x7, local copies, waits for them, and re-layouts, fine_padded(): padded = padded.at[:, place_x, place_y, place_z].set(values)  18.1 us
    ppermute x5, starting transfers between devices, from_behind(): return lax.ppermute(block, axis, route)  17.9 us
    ppermute x5, waiting for transfers between devices, from_behind(): return lax.ppermute(block, axis, route)  16 us
    concatenate x18, other arithmetic, pair_taps(): gathered_taps = jnp.concatenate(pieces, axis=-1)  12.8 us
  transfers between devices with their start and end apart: 11, of which 8 were waited for; matrix products, arithmetic and copies ran while one was open for 3% of the time, Pallas kernels for 0%

profile of v1, /device:TPU:2, one launch (start us, length us, event | category | flops | bytes accessed | tf_op | source)
XLA Modules:
  0.0 616.2 jit_solution(15171440200311305042)
XLA Ops:
  7.2 1.8 copy_convert_fusion
  10.0 3.8 collective-permute-start
  15.8 9.5 %collective-permute-done = bf16[24,3,4,256]{3,0,2,1:T(8,128)(2,1)S(1)} collective-permute-done((bf16[24,3,4,256]{3,0,2,1:T(8,128)(2,1)S(1)}, bf16[24,3,4,256]{3,0,2,1:T(8,128)(2,1)S(1)}, u32[]{:S(2)}, u32[]{:S(2)}) %collective-permute-start) | collective-permute-done | bytes 147488 | tf_op jit(solution)/shard_map/ppermute | solution.py:23
  32.3 7.6 %scatter.196 = bf16[24,5,5,5,64]{4,3,0,2,1:T(8,128)(2,1)S(1)} dynamic-update-slice(bf16[24,5,5,5,64]{4,3,0,2,1:T(8,128)(2,1)S(1)} %pad.247, bf16[24,4,4,1,64]{4,3,0,2,1:T(2,128)(2,1)S(1)} %copy.350, s32[]{:T(128)} %constant.1608.clone.1, s32[]{:T(128)} %constant.1614.clone.1, s32[]{:T(128)} %constant.1614.clone.1, s32[]{:T(128)} %constant.1608.clone.1, s32[]{:T(128)} %constant.1608.clone.1) | dynamic-update-slice | bytes 98308 | tf_op jit(solution)/shard_map/scatter | solution.py:70
  39.9 3.1 scatter.199
  44.7 3.4 scatter.201
  48.2 1.9 scatter.204
  62.0 3.6 collective-permute-start.1
  69.1 5.8 collective-permute-start.3
  74.8 1.9 collective-permute-start.2
  77.5 6.5 %collective-permute-done.2 = bf16[6,6,4,512]{3,2,0,1:T(4,128)(2,1)S(1)} collective-permute-done((bf16[6,6,4,512]{3,2,0,1:T(4,128)(2,1)S(1)}, bf16[6,6,4,512]{3,2,0,1:T(4,128)(2,1)S(1)}, u32[]{:S(2)}, u32[]{:S(2)}) %collective-permute-start.2) | collective-permute-done | bytes 147488 | tf_op jit(solution)/shard_map/ppermute | solution.py:14
  113.0 2.0 pad_maximum_fusion.7
  116.8 1.8 pad_maximum_fusion.8
  123.6 2.1 collective-permute-start.4
  142.6 6.4 %collective-permute-start.5 = (bf16[1,2,2,256]{3,2,1,0:T(2,128)(2,1)S(1)}, bf16[1,2,2,256]{3,2,1,0:T(2,128)(2,1)S(1)}, u32[]{:S(2)}, u32[]{:S(2)}) collective-permute-start(bf16[1,2,2,256]{3,2,1,0:T(2,128)(2,1)S(1)} %slice.3357), channel_id=1, source_target_pairs={{1,0},{2,1},{3,2},{4,3},{5,4},{6,5},{7,6},{8,7},{9,8},{10,9},{11,1... | collective-permute-start | bytes 6152 | tf_op jit(solution)/shard_map/ppermute | solution.py:23
  152.0 6.3 %collective-permute-start.7 = (bf16[6,6,4,512]{3,2,0,1:T(4,128)(2,1)S(1)}, bf16[6,6,4,512]{3,2,0,1:T(4,128)(2,1)S(1)}, u32[]{:S(2)}, u32[]{:S(2)}) collective-permute-start(bf16[6,6,4,512]{3,2,0,1:T(4,128)(2,1)S(1)} %constant_dynamic-update-slice_fusion.36), channel_id=1, source_target_pairs={{1,0},{2,1},{3,2},{4,3},{5,4},{6,5},{7,6},{8,7},{9,8},{10,9},{11,1... | collective-permute-start | bytes 442376 | tf_op jit(solution)/shard_map/ppermute | solution.py:15
  158.3 1.9 collective-permute-start.6
  163.8 3.7 collective-permute-done.6
  226.9 1.9 pad_maximum_fusion.16
  229.8 1.8 pad_maximum_fusion.17
  238.0 1.9 collective-permute-start.8
  241.0 4.7 collective-permute-done.8
  248.1 274.0 %all-reduce.8.cloned.1.call-done = (f32[221184]{0:T(1024)}, f32[442368]{0:T(1024)}, f32[65536]{0:T(1024)}) async-done(((f32[221184]{0:T(1024)}, f32[442368]{0:T(1024)}, f32[65536]{0:T(1024)}), (f32[221184]{0:T(1024)}, f32[442368]{0:T(1024)}, f32[65536]{0:T(1024)})) %all-reduce.8.cloned.1.call-update) | async-done | bytes 2916368 | tf_op jit(solution)/shard_map/psum | solution.py:349
  524.1 81.0 %all-reduce.10.cloned.1.call-done = (f32[221184]{0:T(1024)}, f32[442368]{0:T(1024)}, f32[65536]{0:T(1024)}) async-done(((f32[221184]{0:T(1024)}, f32[442368]{0:T(1024)}, f32[65536]{0:T(1024)}), (f32[221184]{0:T(1024)}, f32[442368]{0:T(1024)}, f32[65536]{0:T(1024)})) %all-reduce.10.cloned.1.call-update) | async-done | bytes 2916368 | tf_op jit(solution)/shard_map/psum | solution.py:348
  (638 shorter events, 159.6 us)
Async XLA Ops:
  7.2 514.9 %all-reduce.8.cloned.1.call-start = ((), (), s32[]{:S(2)}) async-start(), calls=%async_computation | async-start | bytes 5832704 | tf_op jit(solution)/shard_map/psum | solution.py:349
  10.0 15.2 %collective-permute-start = (bf16[24,3,4,256]{3,0,2,1:T(8,128)(2,1)S(1)}, bf16[24,3,4,256]{3,0,2,1:T(8,128)(2,1)S(1)}, u32[]{:S(2)}, u32[]{:S(2)}) collective-permute-start(bf16[24,3,4,256]{3,0,2,1:T(8,128)(2,1)S(1)} %constant_dynamic-update-slice_fusion), channel_id=1, source_target_pairs={{0,1},{1,2},{2,3},{3,4},{4,5},{5,6},{6,7},{7,8},{8,9},{9,10},{10,1... | collective-permute-start | bytes 442376 | tf_op jit(solution)/shard_map/ppermute | solution.py:23
  15.0 76.9 %copy-start.45 = (s32[1024]{0:T(1024)}, s32[1024]{0:T(1024)S(1)}, u32[]{:S(2)}) copy-start(s32[1024]{0:T(1024)S(1)} %get-tuple-element.874) | copy-start | bytes 12292
  15.0 77.6 %copy-start.48 = (s32[1024]{0:T(1024)}, s32[1024]{0:T(1024)S(1)}, u32[]{:S(2)}) copy-start(s32[1024]{0:T(1024)S(1)} %get-tuple-element.873) | copy-start | bytes 12292
  15.0 78.3 %copy-start.47 = (s32[1024]{0:T(1024)}, s32[1024]{0:T(1024)S(1)}, u32[]{:S(2)}) copy-start(s32[1024]{0:T(1024)S(1)} %get-tuple-element.872) | copy-start | bytes 12292
  15.1 79.1 %copy-start.50 = (s32[1024]{0:T(1024)}, s32[1024]{0:T(1024)S(1)}, u32[]{:S(2)}) copy-start(s32[1024]{0:T(1024)S(1)} %get-tuple-element.871) | copy-start | bytes 12292
  15.1 79.8 %copy-start.49 = (s32[1024]{0:T(1024)}, s32[1024]{0:T(1024)S(1)}, u32[]{:S(2)}) copy-start(s32[1024]{0:T(1024)S(1)} %get-tuple-element.870) | copy-start | bytes 12292
  15.1 80.6 %copy-start.52 = (s32[1024]{0:T(1024)}, s32[1024]{0:T(1024)S(1)}, u32[]{:S(2)}) copy-start(s32[1024]{0:T(1024)S(1)} %get-tuple-element.869) | copy-start | bytes 12292
  15.1 81.3 %copy-start.51 = (s32[1024]{0:T(1024)}, s32[1024]{0:T(1024)S(1)}, u32[]{:S(2)}) copy-start(s32[1024]{0:T(1024)S(1)} %get-tuple-element.868) | copy-start | bytes 12292
  15.1 82.0 %copy-start.54 = (s32[1024]{0:T(1024)}, s32[1024]{0:T(1024)S(1)}, u32[]{:S(2)}) copy-start(s32[1024]{0:T(1024)S(1)} %get-tuple-element.867) | copy-start | bytes 12292
  15.1 82.7 %copy-start.53 = (s32[1024]{0:T(1024)}, s32[1024]{0:T(1024)S(1)}, u32[]{:S(2)}) copy-start(s32[1024]{0:T(1024)S(1)} %get-tuple-element.866) | copy-start | bytes 12292
  15.2 83.4 %copy-start.56 = (s32[1024]{0:T(1024)}, s32[1024]{0:T(1024)S(1)}, u32[]{:S(2)}) copy-start(s32[1024]{0:T(1024)S(1)} %get-tuple-element.865) | copy-start | bytes 12292
  15.2 84.1 %copy-start.55 = (s32[1024]{0:T(1024)}, s32[1024]{0:T(1024)S(1)}, u32[]{:S(2)}) copy-start(s32[1024]{0:T(1024)S(1)} %get-tuple-element.864) | copy-start | bytes 12292
  15.8 84.3 %copy-start.58 = (s32[1024]{0:T(1024)}, s32[1024]{0:T(1024)S(1)}, u32[]{:S(2)}) copy-start(s32[1024]{0:T(1024)S(1)} %get-tuple-element.863) | copy-start | bytes 12292
  15.8 85.0 %copy-start.57 = (s32[1024]{0:T(1024)}, s32[1024]{0:T(1024)S(1)}, u32[]{:S(2)}) copy-start(s32[1024]{0:T(1024)S(1)} %get-tuple-element.862) | copy-start | bytes 12292
  62.0 5.5 collective-permute-start.1
  69.1 8.4 %collective-permute-start.3 = (bf16[6,6,4,512]{3,2,0,1:T(4,128)(2,1)S(1)}, bf16[6,6,4,512]{3,2,0,1:T(4,128)(2,1)S(1)}, u32[]{:S(2)}, u32[]{:S(2)}) collective-permute-start(bf16[6,6,4,512]{3,2,0,1:T(4,128)(2,1)S(1)} %constant_dynamic-update-slice_fusion.30), channel_id=1, source_target_pairs={{1,0},{2,1},{3,2},{4,3},{5,4},{6,5},{7,6},{8,7},{9,8},{10,9},{11,1... | collective-permute-start | bytes 442376 | tf_op jit(solution)/shard_map/ppermute | solution.py:15
  74.8 9.1 %collective-permute-start.2 = (bf16[6,6,4,512]{3,2,0,1:T(4,128)(2,1)S(1)}, bf16[6,6,4,512]{3,2,0,1:T(4,128)(2,1)S(1)}, u32[]{:S(2)}, u32[]{:S(2)}) collective-permute-start(bf16[6,6,4,512]{3,2,0,1:T(4,128)(2,1)S(1)} %constant_dynamic-update-slice_fusion.30), channel_id=1, source_target_pairs={{0,1},{1,2},{2,3},{3,4},{4,5},{5,6},{6,7},{7,8},{8,9},{9,10},{10,1... | collective-permute-start | bytes 442376 | tf_op jit(solution)/shard_map/ppermute | solution.py:14
  123.6 15.2 %collective-permute-start.4 = (bf16[8,2,2,256]{3,0,2,1:T(8,128)(2,1)S(1)}, bf16[8,2,2,256]{3,0,2,1:T(8,128)(2,1)S(1)}, u32[]{:S(2)}, u32[]{:S(2)}) collective-permute-start(bf16[8,2,2,256]{3,0,2,1:T(8,128)(2,1)S(1)} %bitcast.517), channel_id=1, source_target_pairs={{0,1},{1,2},{2,3},{3,4},{4,5},{5,6},{6,7},{7,8},{8,9},{9,10},{10,1... | collective-permute-start | bytes 49160 | tf_op jit(solution)/shard_map/ppermute | solution.py:23
  142.6 7.5 %collective-permute-start.5 = (bf16[1,2,2,256]{3,2,1,0:T(2,128)(2,1)S(1)}, bf16[1,2,2,256]{3,2,1,0:T(2,128)(2,1)S(1)}, u32[]{:S(2)}, u32[]{:S(2)}) collective-permute-start(bf16[1,2,2,256]{3,2,1,0:T(2,128)(2,1)S(1)} %slice.3357), channel_id=1, source_target_pairs={{1,0},{2,1},{3,2},{4,3},{5,4},{6,5},{7,6},{8,7},{9,8},{10,9},{11,1... | collective-permute-start | bytes 6152 | tf_op jit(solution)/shard_map/ppermute | solution.py:23
  152.0 11.8 %collective-permute-start.7 = (bf16[6,6,4,512]{3,2,0,1:T(4,128)(2,1)S(1)}, bf16[6,6,4,512]{3,2,0,1:T(4,128)(2,1)S(1)}, u32[]{:S(2)}, u32[]{:S(2)}) collective-permute-start(bf16[6,6,4,512]{3,2,0,1:T(4,128)(2,1)S(1)} %constant_dynamic-update-slice_fusion.36), channel_id=1, source_target_pairs={{1,0},{2,1},{3,2},{4,3},{5,4},{6,5},{7,6},{8,7},{9,8},{10,9},{11,1... | collective-permute-start | bytes 442376 | tf_op jit(solution)/shard_map/ppermute | solution.py:15
  158.3 9.1 %collective-permute-start.6 = (bf16[6,6,4,512]{3,2,0,1:T(4,128)(2,1)S(1)}, bf16[6,6,4,512]{3,2,0,1:T(4,128)(2,1)S(1)}, u32[]{:S(2)}, u32[]{:S(2)}) collective-permute-start(bf16[6,6,4,512]{3,2,0,1:T(4,128)(2,1)S(1)} %constant_dynamic-update-slice_fusion.36), channel_id=1, source_target_pairs={{0,1},{1,2},{2,3},{3,4},{4,5},{5,6},{6,7},{7,8},{8,9},{9,10},{10,1... | collective-permute-start | bytes 442376 | tf_op jit(solution)/shard_map/ppermute | solution.py:14
  238.0 7.7 %collective-permute-start.8 = (bf16[8,2,2,256]{3,0,2,1:T(8,128)(2,1)S(1)}, bf16[8,2,2,256]{3,0,2,1:T(8,128)(2,1)S(1)}, u32[]{:S(2)}, u32[]{:S(2)}) collective-permute-start(bf16[8,2,2,256]{3,0,2,1:T(8,128)(2,1)S(1)} %bitcast.518), channel_id=1, source_target_pairs={{0,1},{1,2},{2,3},{3,4},{4,5},{5,6},{6,7},{7,8},{8,9},{9,10},{10,1... | collective-permute-start | bytes 49160 | tf_op jit(solution)/shard_map/ppermute | solution.py:23
  248.0 357.1 %all-reduce.10.cloned.1.call-start = ((), (), s32[]{:S(2)}) async-start(), calls=%async_computation.1 | async-start | bytes 5832704 | tf_op jit(solution)/shard_map/psum | solution.py:348
  (59 other events, 920.9 us)
Sparse Core Ops, SparseCore 0:
  248.1 273.8 all-reduce.7
  524.8 80.2 all-reduce.9
